TPU v7x, 32 devices: a whole 2x2x4 slice. The times are simulated.
32 devices in a mesh: band: 8 (over z, x), lev: 4 (over y, core).
Axes of the slice: x: 2, y: 2, z: 4, core: 2. Of those that a mesh axis runs over, the one named last changes fastest.
Arguments:
- columns: bfloat16 [65536, 274], P(('band', 'lev')), may hold values from -6 to 6
- departures: bfloat16 [4, 256, 128, 616], P('lev', 'band'), may hold values from -6 to 6
- jacobian: bfloat16 [274, 616], replicated, may hold values from -0.375 to 0.375
- chan_precision: bfloat16 [616, 616], replicated, as said below
- send_rows: int32 [32, 32, 4], P(('band', 'lev')), may hold values from 0 to 2047
- obs_slot: int32 [4, 256, 128], P('lev', 'band'), may hold values from 0 to 127
- counts: int32 [4, 256], P('lev', 'band'), may hold values from 16 to 128, as said below
Outputs:
- column_gradient: float32 [65536, 274], P(('band', 'lev'))
Inputs may be any that keep to these rules, and one draw needn't show every extreme that they name: `send_rows`: each entry names a column of the sending device. `obs_slot`: each entry names one of the 128 slots, ordered by sending device then place. `counts`: each entry is 128 divided by 1, 2, 4 or 8; some entry equals 128. `chan_precision`: symmetric positive definite.
All inputs are finite; a program needn't handle non-finite values.
Results may differ from a plain program's by a relative error of at most 0.0018.
Values may be sent and summed in bfloat16 or wider, within the bound.
A program may use at most 128 MiB of HBM per device.

v0:
```python
import math

import jax
import jax.numpy as jnp
from jax import lax
from jax.sharding import PartitionSpec as P

corr_length = 2.0


def extended(cells, sides, width):
    for axis, dim in sides:
        count = lax.axis_size(axis)
        ends = count - 1
        head = lax.slice_in_dim(cells, 0, width, axis=dim)
        tail = lax.slice_in_dim(cells, cells.shape[dim] - width, cells.shape[dim], axis=dim)
        cells = jnp.concatenate(
            [
                lax.ppermute(tail, axis, [(i, (i + 1) % count) for i in range(ends)]),
                cells,
                lax.ppermute(head, axis, [((i + 1) % count, i) for i in range(ends)]),
            ],
            axis=dim,
        )
    return cells


def on_device(columns, departures, jacobian, chan_precision, send_rows, obs_slot, counts):
    decay_rate = math.exp(-1.0 / corr_length)
    norm_factor = 1.0 / (1.0 - decay_rate * decay_rate)
    n_band = lax.axis_size("band")
    n_lev = lax.axis_size("lev")
    send_plan = send_rows[0]
    slot_depth = send_plan.shape[1]
    n_slots = send_plan.shape[0] * slot_depth
    prof_width = columns.shape[1]
    outgoing = columns[send_plan].reshape(n_band, n_lev, slot_depth, prof_width)
    arrived = lax.all_to_all(
        lax.all_to_all(outgoing, "band", split_axis=0, concat_axis=0, tiled=True),
        "lev",
        split_axis=1,
        concat_axis=1,
        tiled=True,
    )
    arrived_rows = arrived.reshape(n_slots, prof_width)
    line_deps = departures[0]
    n_lines, n_positions, n_chan = line_deps.shape
    slot_list = obs_slot[0].reshape(-1)
    obs_columns = arrived_rows[slot_list]
    model_equiv = jnp.dot(obs_columns, jacobian, preferred_element_type=jnp.float32)
    valid_mask = jnp.arange(n_positions, dtype=jnp.int32)[None, :] < counts[0][:, None]
    residual = jnp.where(
        valid_mask.reshape(-1, 1),
        model_equiv - line_deps.reshape(-1, n_chan).astype(jnp.float32),
        0.0,
    )
    residual = residual.astype(jnp.bfloat16)
    weighted = jnp.dot(residual, chan_precision, preferred_element_type=jnp.float32).reshape(
        n_lines, n_positions, n_chan
    )
    padded = extended(weighted, (("band", 0),), 1)
    previous = padded[:-2]
    following = padded[2:]
    global_line = lax.axis_index("band") * n_lines + jnp.arange(n_lines, dtype=jnp.int32)
    chain_length = n_band * n_lines
    at_end = (global_line == 0) | (global_line == chain_length - 1)
    chain_diag = jnp.where(at_end, norm_factor, (1.0 + decay_rate * decay_rate) * norm_factor)
    scaled = chain_diag[:, None, None] * weighted - decay_rate * norm_factor * (
        previous + following
    )
    scaled = jnp.where(valid_mask[:, :, None], scaled, 0.0).astype(jnp.bfloat16).reshape(-1, n_chan)
    obs_adjoint = lax.dot_general(
        scaled, jacobian, (((1,), (1,)), ((), ())), preferred_element_type=jnp.float32
    )
    adjoint_slots = jax.ops.segment_sum(obs_adjoint, slot_list, num_segments=n_slots)
    adjoint_slots = adjoint_slots.reshape(n_band, n_lev, slot_depth, prof_width)
    returned = lax.all_to_all(
        lax.all_to_all(adjoint_slots, "band", split_axis=0, concat_axis=0, tiled=True),
        "lev",
        split_axis=1,
        concat_axis=1,
        tiled=True,
    )
    return jax.ops.segment_sum(
        returned.reshape(n_slots, prof_width), send_plan.reshape(-1), num_segments=columns.shape[0]
    )


def solution(mesh):
    placed = (
        P(("band", "lev"), None),
        P("lev", "band", None, None),
        P(),
        P(),
        P(("band", "lev"), None, None),
        P("lev", "band", None),
        P("lev", "band"),
    )
    return jax.shard_map(
        on_device, mesh=mesh, in_specs=placed, out_specs=P(("band", "lev"), None), check_vma=False
    )
```

profile of v0, /device:TPU:0, one launch (start us, length us, event | category | flops | bytes accessed | tf_op | source)
XLA Modules:
  0.0 149.4 jit_solution(4565929134558031174)
XLA Ops:
  0.0 1.9 %copy.23 = bf16[2048,274]{1,0:T(8,128)(2,1)S(1)} copy(bf16[2048,274]{0,1:T(8,128)(2,1)} %param.7) | data formatting | bytes 2244608 | tf_op args[0]
  1.9 0.7 compare_select_fusion.1
  2.6 0.1 copy.22
  2.7 0.1 reshape.134
  2.8 0.9 gather_fusion
  3.6 0.7 reshape.125
  4.3 7.3 %all-to-all-start = ((bf16[8,4,4,274]{3,2,1,0:T(4,128)(2,1)}), bf16[8,4,4,274]{3,2,1,0:T(4,128)(2,1)S(1)}, u32[]{:S(2)}, u32[]{:S(2)}) async-start(bf16[8,4,4,274]{3,2,1,0:T(4,128)(2,1)} %reshape.125), calls=%async_computation | async-start | bytes 196608 | tf_op jit(solution)/shard_map/all_to_all | solution.py:39
  11.6 0.7 compare_select_fusion
  12.3 6.4 %all-to-all-done = bf16[8,4,4,274]{3,2,1,0:T(4,128)(2,1)S(1)} async-done(((bf16[8,4,4,274]{3,2,1,0:T(4,128)(2,1)}), bf16[8,4,4,274]{3,2,1,0:T(4,128)(2,1)S(1)}, u32[]{:S(2)}, u32[]{:S(2)}) %all-to-all-start) | async-done | bytes 70176 | tf_op jit(solution)/shard_map/all_to_all | solution.py:39
  18.7 0.7 copy.24
  19.4 3.3 %all-to-all-start.1 = ((bf16[8,4,4,274]{3,2,0,1:T(4,128)(2,1)}), bf16[8,4,4,274]{3,2,0,1:T(4,128)(2,1)S(1)}, u32[]{:S(2)}, u32[]{:S(2)}) async-start(bf16[8,4,4,274]{3,2,0,1:T(4,128)(2,1)} %copy.24), calls=%async_computation.1 | async-start | bytes 196608 | tf_op jit(solution)/shard_map/all_to_all | solution.py:38
  22.7 0.7 iota_compare_fusion
  23.4 7.6 %copy.26 = f32[1,32,128,616]{2,1,3,0:T(8,128)} copy(bf16[1,32,128,616]{2,3,1,0:T(8,128)(2,1)} %param.8) | data formatting | bytes 15138816 | tf_op jit(solution)/shard_map/convert_element_type | solution.py:54
  31.2 17.0 %gather_fusion.1 = bf16[4096,274]{1,0:T(8,128)(2,1)} fusion(bf16[128,274]{1,0:T(8,128)(2,1)S(1)} %reshape.126, s32[4096]{0:T(1024)S(1)} %broadcast_clamp_fusion), kind=kCustom, calls=%fused_computation.1 | custom fusion | bytes 4505600 | tf_op jit(solution)/shard_map/gather | solution.py:49
  48.2 16.3 %fusion.12 = f32[4096,616]{0,1:T(8,128)} fusion(bf16[616,616]{1,0:T(8,128)(2,1)S(1)} %copy-done, f32[77,8,32,128]{3,2,1,0:T(8,128)} %bitcast.44, bf16[4096,274]{1,0:T(8,128)(2,1)} %gather_fusion.1, bf16[274,616]{1,0:T(8,128)(2,1)S(1)} %copy-done.2, pred[4096]{0:T(1024)(128)(4,1)S(1)} %get-tuple-element.8), kind=kOutput, calls=%fused_computation.19 | convolution fusion | flops 4498751488 | bytes 23530272 | tf_op jit(solution)/shard_map/dot_general | solution.py:58
  64.5 1.1 slice_bitcast_fusion.1
  65.7 2.2 %collective-permute-start = (f32[1,128,616]{1,2,0:T(8,128)S(1)}, f32[1,128,616]{1,2,0:T(8,128)S(1)}, u32[]{:S(2)}, u32[]{:S(2)}) collective-permute-start(f32[1,128,616]{1,2,0:T(8,128)S(1)} %get-tuple-element.5), channel_id=1, source_target_pairs={{0,4},{4,8},{8,12},{12,16},{16,20},{20,24},{24,28},{1,5},{5,9},{9,... | collective-permute-start | bytes 946184 | tf_op jit(solution)/shard_map/ppermute | solution.py:19
  67.9 1.5 collective-permute-start.1
  69.4 6.1 %copy.35 = f32[77,8,32,128]{3,2,1,0:T(8,128)S(1)} copy(f32[77,8,32,128]{3,1,2,0:T(8,128)} %bitcast.43) | data formatting | bytes 20185088
  75.5 6.4 %collective-permute-done = f32[1,128,616]{1,2,0:T(8,128)S(1)} collective-permute-done((f32[1,128,616]{1,2,0:T(8,128)S(1)}, f32[1,128,616]{1,2,0:T(8,128)S(1)}, u32[]{:S(2)}, u32[]{:S(2)}) %collective-permute-start) | collective-permute-done | bytes 315424 | tf_op jit(solution)/shard_map/ppermute | solution.py:19
  82.0 5.1 %fusion.6 = bf16[32,128,616]{1,0,2:T(8,128)(2,1)S(1)} fusion(f32[1,128,616]{1,0,2:T(1,128)S(1)} %bitcast.47, f32[32,128,616]{1,0,2:T(8,128)S(1)} %bitcast.42, f32[1,128,616]{1,0,2:T(1,128)S(1)} %bitcast.46, f32[32]{0:T(128)S(1)} %or_select_fusion, pred[32,128]{1,0:T(8,128)(4,1)S(1)} %get-tuple-element.7), kind=kLoop, calls=%fused_computation.12 | loop fusion | flops 20185088 | bytes 15773824 | tf_op jit(solution)/shard_map/convert_element_type | solution.py:71
  87.1 8.3 %fusion.7 = f32[4096,274]{1,0:T(8,128)} fusion(bf16[274,616]{1,0:T(8,128)(2,1)S(1)} %copy-done.2, bf16[77,8,32,128]{3,2,1,0:T(8,128)(2,1)S(1)} %bitcast.45), kind=kOutput, calls=%fused_computation.14 | convolution fusion | flops 1382678528 | bytes 9873056 | tf_op jit(solution)/shard_map/dot_general | solution.py:72
  95.4 25.2 %scatter_custom_fusion = f32[128,274]{1,0:T(8,128)S(1)} fusion(s32[4096]{0:T(1024)} %bitcast.50, f32[4096,274]{1,0:T(8,128)} %fusion.7, f32[]{:T(128)} %constant.11.clone.1), kind=kCustom, calls=%fused_computation.22 | custom fusion | flops 1122304 | bytes 140800 | tf_op jit(solution)/shard_map/scatter-add | solution.py:75
  120.6 12.9 %all_to_all.20 = f32[8,4,4,274]{3,2,1,0:T(4,128)S(1)} all-to-all(f32[8,4,4,274]{3,2,1,0:T(4,128)S(1)} %reshape.129), channel_id=1, replica_groups=mesh['band'=8,'lev'=4] {'band'}, dimensions={0} | all-to-all | bytes 280576 | tf_op jit(solution)/shard_map/all_to_all | solution.py:78
  133.5 0.7 copy.30
  134.2 3.4 %all-to-all-start.3 = ((f32[8,4,4,274]{3,2,0,1:T(4,128)}), f32[8,4,4,274]{3,2,0,1:T(4,128)S(1)}, u32[]{:S(2)}, u32[]{:S(2)}) async-start(f32[8,4,4,274]{3,2,0,1:T(4,128)} %copy.30), calls=%async_computation.3 | async-start | bytes 393216 | tf_op jit(solution)/shard_map/all_to_all | solution.py:77
  137.5 0.1 copy.21
  137.6 0.1 reshape.158
  137.7 5.1 %all-to-all-done.3 = f32[8,4,4,274]{3,2,0,1:T(4,128)S(1)} async-done(((f32[8,4,4,274]{3,2,0,1:T(4,128)}), f32[8,4,4,274]{3,2,0,1:T(4,128)S(1)}, u32[]{:S(2)}, u32[]{:S(2)}) %all-to-all-start.3) | async-done | bytes 140320 | tf_op jit(solution)/shard_map/all_to_all | solution.py:77
  142.9 0.1 reshape.160
  142.9 3.1 %scatter_custom_fusion.1 = f32[2048,274]{1,0:T(8,128)} fusion(s32[128]{0:T(128)S(1)} %reshape.158, f32[128,274]{1,0:T(8,128)S(1)} %reshape.160, f32[]{:T(128)} %constant.11.clone.1), kind=kCustom, calls=%fused_computation.17 | custom fusion | flops 35072 | bytes 2244612 | tf_op jit(solution)/shard_map/scatter-add | solution.py:84
  146.1 3.3 %copy.32 = f32[2048,274]{0,1:T(8,128)} copy(f32[2048,274]{1,0:T(8,128)} %scatter_custom_fusion.1) | data formatting | bytes 4489216 | tf_op jit(solution)/shard_map/scatter-add | solution.py:84
  (15 shorter events, 0.2 us)
Async XLA Ops:
  0.0 48.2 %copy-start = (bf16[616,616]{1,0:T(8,128)(2,1)S(1)}, bf16[616,616]{1,0:T(8,128)(2,1)}, u32[]{:S(2)}) copy-start(bf16[616,616]{1,0:T(8,128)(2,1)} %param.10) | copy-start | bytes 2276740
  4.3 14.4 %all-to-all-start = ((bf16[8,4,4,274]{3,2,1,0:T(4,128)(2,1)}), bf16[8,4,4,274]{3,2,1,0:T(4,128)(2,1)S(1)}, u32[]{:S(2)}, u32[]{:S(2)}) async-start(bf16[8,4,4,274]{3,2,1,0:T(4,128)(2,1)} %reshape.125), calls=%async_computation | async-start | bytes 196608 | tf_op jit(solution)/shard_map/all_to_all | solution.py:39
  19.4 11.7 %all-to-all-start.1 = ((bf16[8,4,4,274]{3,2,0,1:T(4,128)(2,1)}), bf16[8,4,4,274]{3,2,0,1:T(4,128)(2,1)S(1)}, u32[]{:S(2)}, u32[]{:S(2)}) async-start(bf16[8,4,4,274]{3,2,0,1:T(4,128)(2,1)} %copy.24), calls=%async_computation.1 | async-start | bytes 196608 | tf_op jit(solution)/shard_map/all_to_all | solution.py:38
  31.2 17.1 %copy-start.2 = (bf16[274,616]{1,0:T(8,128)(2,1)S(1)}, bf16[274,616]{1,0:T(8,128)(2,1)}, u32[]{:S(2)}) copy-start(bf16[274,616]{1,0:T(8,128)(2,1)} %param.9) | copy-start | bytes 1012708
  65.7 16.3 %collective-permute-start = (f32[1,128,616]{1,2,0:T(8,128)S(1)}, f32[1,128,616]{1,2,0:T(8,128)S(1)}, u32[]{:S(2)}, u32[]{:S(2)}) collective-permute-start(f32[1,128,616]{1,2,0:T(8,128)S(1)} %get-tuple-element.5), channel_id=1, source_target_pairs={{0,4},{4,8},{8,12},{12,16},{16,20},{20,24},{24,28},{1,5},{5,9},{9,... | collective-permute-start | bytes 946184 | tf_op jit(solution)/shard_map/ppermute | solution.py:19
  67.9 14.1 %collective-permute-start.1 = (f32[1,128,616]{1,2,0:T(8,128)S(1)}, f32[1,128,616]{1,2,0:T(8,128)S(1)}, u32[]{:S(2)}, u32[]{:S(2)}) collective-permute-start(f32[1,128,616]{1,2,0:T(8,128)S(1)} %get-tuple-element.6), channel_id=1, source_target_pairs={{4,0},{8,4},{12,8},{16,12},{20,16},{24,20},{28,24},{5,1},{9,5},{13... | collective-permute-start | bytes 946184 | tf_op jit(solution)/shard_map/ppermute | solution.py:21
  87.0 50.5 %copy-start.1 = (s32[1,32,4]{1,2,0:T(4,128)S(1)}, s32[1,32,4]{1,2,0:T(4,128)}, u32[]{:S(2)}) copy-start(s32[1,32,4]{1,2,0:T(4,128)} %param.11) | copy-start | bytes 1540
  134.2 8.7 %all-to-all-start.3 = ((f32[8,4,4,274]{3,2,0,1:T(4,128)}), f32[8,4,4,274]{3,2,0,1:T(4,128)S(1)}, u32[]{:S(2)}, u32[]{:S(2)}) async-start(f32[8,4,4,274]{3,2,0,1:T(4,128)} %copy.30), calls=%async_computation.3 | async-start | bytes 393216 | tf_op jit(solution)/shard_map/all_to_all | solution.py:77
where the time goes:
time: 150 us; the launch traced here: 149 us
  local copies, waits for them, and re-layouts  40.7 us (27%)
  other arithmetic  35.5 us (24%)
  matrix products  24.6 us (16%)
  waiting for transfers between devices  17.9 us (12%)
  starting transfers between devices  17.6 us (12%)
  blocking collectives  12.9 us (9%)
    scatter-add x1, other arithmetic, on_device(): jax.ops.segment_sum(obs_adjoint, slot_list, num_segments=n_slots)  25.2 us
    gather x1, local copies, waits for them, and re-layouts, on_device(): obs_columns = arrived_rows[slot_list]  17 us
    dot_general x1, matrix products, on_device(): jnp.dot(residual, chan_precision, preferred_element_type=jnp.float32)  16.3 us
    all_to_all x1, blocking collectives, on_device(): lax.all_to_all(adjoint_slots, 'band', split_axis=0, concat_axis=0, tiled=...  12.9 us
    dot_general x1, matrix products, on_device(): lax.dot_general(scaled, jacobian, (((1,), (1,)), ((), ())), preferred_ele...  8.3 us
    unnamed x9, local copies, waits for them, and re-layouts  8.11 us
    convert_element_type x1, local copies, waits for them, and re-layouts, on_device(): line_deps.reshape(-1, n_chan).astype(jnp.float32)  7.65 us
    all_to_all x1, starting transfers between devices, on_device(): lax.all_to_all(outgoing, 'band', split_axis=0, concat_axis=0, tiled=True)  7.25 us
  transfers between devices with their start and end apart: 5, of which 3 were waited for; matrix products, arithmetic and copies ran while one was open for 10% of the time, Pallas kernels for 0%

commit v1 on v0

v1 whole, which is shorter than its diff:
```python
import functools
import math

import jax
import jax.numpy as jnp
from jax import lax
from jax.experimental import pallas as pl
from jax.experimental.pallas import tpu as pltpu
from jax.sharding import PartitionSpec as P

MESH = pl.DeviceIdType.MESH
corr_length = 2.0
F32, BF16 = jnp.float32, jnp.bfloat16


def halves(value):
    high = value.astype(BF16)
    return high, (value - high.astype(F32)).astype(BF16)


def across(left, right):
    return lax.dot_general(left, right, (((1,), (1,)), ((), ())), preferred_element_type=F32)


def plain(left, right):
    return jnp.dot(left, right, preferred_element_type=F32)


def hot(row, count):
    return jnp.where(lax.broadcasted_iota(jnp.int32, (count, row.shape[1]), 0) == row, 1.0, 0.0)


def picks(rows_ref, n_cols):
    n, cap = rows_ref.shape
    lanes = lax.broadcasted_iota(jnp.int32, (n, n_cols), 1)
    return jnp.concatenate(
        [jnp.where(lanes == rows_ref[:, c : c + 1], 1.0, 0.0) for c in range(cap)], axis=0
    ).astype(BF16)


def exchange(
    n_band, n_lev, group, cols, dep, jac, prec, rows, slots, counts, back,
    lines, padded, edge, edge_in, dep_in, wide, sent, got, gotf, mine, mine_in,
    obs, pair, small, total, dep_sem, entry_out, entry_in, col_out, col_in, row_out, row_in, adj_out, adj_in,
):
    decay = math.exp(-1.0 / corr_length)
    norm = 1.0 / (1.0 - decay * decay)
    inner, side = (1.0 + decay * decay) * norm, decay * norm
    n = n_band * n_lev
    n_lines, n_chan, n_pos = dep.shape
    cap, prof = sent.shape[1], sent.shape[2]
    n_slots = n * cap
    band, lev = lax.axis_index("band"), lax.axis_index("lev")
    me = band * n_lev + lev
    has_prev, has_next = band > 0, band < n_band - 1

    barrier = pltpu.get_barrier_semaphore()

    def greet(step, carry):
        other = lax.rem(me + step, n)
        pl.semaphore_signal(
            barrier, inc=1, device_id=(other // n_lev, lax.rem(other, n_lev)), device_id_type=MESH
        )
        return carry

    lax.fori_loop(1, n, greet, 0)

    n_groups = n_lines // group

    def load(g):
        part = pl.ds(g * group, group)
        return pltpu.make_async_copy(dep.at[part], lines.at[part], dep_sem.at[g])

    for g in range(n_groups):
        load(g).start()

    gathered = across(picks(rows, cols.shape[1]), cols[...])
    for c in range(cap):
        wide[:, c, :] = gathered[c * n : (c + 1) * n]
    sent[...] = wide[...].astype(BF16)
    got[me] = sent[me]

    numbers = slots[...]
    ordered = lax.rem(numbers, cap) * n + lax.div(numbers, cap)
    place = lax.broadcasted_iota(jnp.int32, (n_lines, n_pos), 1)
    ordered = jnp.where(place < counts[...], ordered, -1)
    nothing = jnp.full((8, n_pos), -1, jnp.int32)
    padded[0:8] = nothing
    padded[8 : 8 + n_lines] = ordered
    padded[8 + n_lines : 16 + n_lines] = nothing
    edge[0] = jnp.broadcast_to(ordered[0:1], (8, n_pos))
    edge[1] = jnp.broadcast_to(ordered[n_lines - 1 : n_lines], (8, n_pos))

    pl.semaphore_wait(barrier, n - 1)

    def scatter(blocks, target, out_sem, in_sem):
        def send(step, carry):
            other = lax.rem(me + step, n)
            pltpu.make_async_remote_copy(
                src_ref=blocks.at[other], dst_ref=target.at[me], send_sem=out_sem, recv_sem=in_sem,
                device_id=(other // n_lev, lax.rem(other, n_lev)), device_id_type=MESH,
            ).start()
            return carry

        lax.fori_loop(1, n, send, 0)

    def settle(blocks, sem):
        others = blocks.at[pl.ds(0, n - 1)]
        pltpu.make_async_copy(others, others, sem).wait()

    scatter(sent, got, col_out, col_in)

    def entries(to):
        line = 0 if to == 0 else n_lines - 1
        other = (band - 1 if to == 0 else band + 1, lev)
        place = 1 - to
        return (
            pltpu.make_async_remote_copy(
                src_ref=dep.at[line], dst_ref=dep_in.at[place], send_sem=entry_out.at[to],
                recv_sem=entry_in.at[place], device_id=other, device_id_type=MESH),
            pltpu.make_async_remote_copy(
                src_ref=edge.at[to], dst_ref=edge_in.at[place], send_sem=entry_out.at[2 + to],
                recv_sem=entry_in.at[2 + place], device_id=other, device_id_type=MESH),
        )

    def columns_to(to):
        other = (band - 1 if to == 0 else band + 1, lev)
        return pltpu.make_async_remote_copy(
            src_ref=mine, dst_ref=mine_in.at[1 - to], send_sem=row_out.at[to],
            recv_sem=row_in.at[1 - to], device_id=other, device_id_type=MESH)

    neighbours = ((0, has_prev), (1, has_next))
    for to, there in neighbours:
        @pl.when(there)
        def _(to=to):
            for copy in entries(to):
                copy.start()

    obs[...] = jnp.zeros_like(obs)
    pair[...] = jnp.zeros_like(pair)

    def add_group(g, carry):
        load(g).wait()
        near = padded[pl.ds(pl.multiple_of(g * group, 8), group + 16)]
        own, both, data = [], [], []
        for j in range(group):
            here = near[8 + j : 9 + j]
            before = jnp.where(here >= 0, near[7 + j : 8 + j], -1)
            after = jnp.where(here >= 0, near[9 + j : 10 + j], -1)
            own.append(hot(here, n_slots).astype(BF16))
            both.append((hot(before, n_slots) + hot(after, n_slots)).astype(BF16))
            data.append(lines[g * group + j])
        own = jnp.concatenate(own, axis=1)
        weights = jnp.concatenate([own, jnp.concatenate(both, axis=1)], axis=0)
        obs[...] += across(jnp.concatenate(data, axis=1), weights)
        pair[...] += across(weights, own)
        return carry

    lax.fori_loop(0, n_groups, add_group, 0)

    obs[:, :n_slots] = inner * obs[:, :n_slots] - side * obs[:, n_slots:]
    pair[:n_slots] = inner * pair[:n_slots] - side * pair[n_slots:]

    for line, at_end in ((0, band == 0), (n_lines - 1, band == n_band - 1)):
        @pl.when(at_end)
        def _(line=line):
            own = hot(padded[8 + line : 9 + line], n_slots).astype(BF16)
            excess = decay * decay * norm
            obs[:, :n_slots] -= excess * across(lines[line], own)
            pair[:n_slots] -= excess * across(own, own)

    for at, there in neighbours:
        @pl.when(there)
        def _(at=at):
            for copy in entries(at):
                copy.wait_send()
            pltpu.make_async_copy(dep_in.at[at], dep_in.at[at], entry_in.at[at]).wait()
            pltpu.make_async_copy(edge_in.at[at], edge_in.at[at], entry_in.at[2 + at]).wait()
            line = 0 if at == 0 else n_lines - 1
            theirs = edge_in[at][0:1]
            row = jnp.where(theirs >= 0, padded[8 + line : 9 + line], -1)
            mask = hot(row, n_slots).astype(BF16)
            obs[:, :n_slots] -= side * across(dep_in[at], mask)
            small[at] = across(mask, hot(theirs, n_slots).astype(BF16)).astype(BF16)

    def two(left, value):
        both = plain(left, jnp.concatenate(halves(value), axis=1))
        width = value.shape[1]
        return both[:, :width] + both[:, width:]

    measured = two(jac[...], two(prec[...], obs[:, :n_slots])).T
    high, low = halves(across(prec[...], jac[...]))
    metric_high, metric_low = halves(plain(jac[...], high) + plain(jac[...], low))
    pair_high, pair_low = halves(pair[:n_slots])

    settle(got, col_in)
    gotf[...] = got[...].astype(F32)
    mine[...] = jnp.concatenate([gotf[:, c, :] for c in range(cap)], axis=0).astype(BF16)
    for to, there in neighbours:
        @pl.when(there)
        def _(to=to):
            columns_to(to).start()
    block = mine[...]
    total[...] = plain(pair_high, block) + plain(pair_low, block)
    for at, there in neighbours:
        @pl.when(there)
        def _(at=at):
            columns_to(at).wait_send()
            pltpu.make_async_copy(mine_in.at[at], mine_in.at[at], row_in.at[at]).wait()
            total[...] -= side * plain(small[at], mine_in[at])
    mixed_high, mixed_low = halves(total[...])
    adjoint = (
        plain(mixed_high, metric_high) + (plain(mixed_low, metric_high) + plain(mixed_high, metric_low)) - measured
    )
    settle(sent, col_out)
    for c in range(cap):
        wide[:, c, :] = adjoint[c * n : (c + 1) * n]
    back[me] = wide[me]
    scatter(wide, back, adj_out, adj_in)
    settle(back, adj_in)
    settle(wide, adj_out)


def spread(back, rows, out):
    n, cap = rows.shape
    values = jnp.concatenate([back[:, c, :] for c in range(cap)], axis=0).T
    chosen = picks(rows, out.shape[1])
    high, low = halves(values)
    out[...] = plain(jnp.concatenate([high, low], axis=1), jnp.concatenate([chosen, chosen], axis=0))


def on_device(columns, departures, jacobian, chan_precision, send_rows, obs_slot, counts):
    n_band, n_lev = lax.axis_size("band"), lax.axis_size("lev")
    n = n_band * n_lev
    rows = send_rows[0]
    cap = rows.shape[1]
    n_slots = n * cap
    n_cols, prof = columns.shape
    dep = departures[0].transpose(0, 2, 1)
    n_lines, n_chan, n_pos = dep.shape
    group = 8
    in_vmem = pl.BlockSpec(memory_space=pltpu.VMEM)
    sem = pltpu.SemaphoreType.DMA
    back = pl.pallas_call(
        functools.partial(exchange, n_band, n_lev, group),
        out_shape=jax.ShapeDtypeStruct((n, cap, prof), F32),
        in_specs=[in_vmem, pl.BlockSpec(memory_space=pl.ANY)] + [in_vmem] * 5,
        out_specs=in_vmem,
        scratch_shapes=[
            pltpu.VMEM((n_lines, n_chan, n_pos), BF16),
            pltpu.VMEM((n_lines + 16, n_pos), jnp.int32),
            pltpu.VMEM((2, 8, n_pos), jnp.int32),
            pltpu.VMEM((2, 8, n_pos), jnp.int32),
            pltpu.VMEM((2, n_chan, n_pos), BF16),
            pltpu.VMEM((n, cap, prof), F32),
            pltpu.VMEM((n, cap, prof), BF16),
            pltpu.VMEM((n, cap, prof), BF16),
            pltpu.VMEM((n, cap, prof), F32),
            pltpu.VMEM((n_slots, prof), BF16),
            pltpu.VMEM((2, n_slots, prof), BF16),
            pltpu.VMEM((n_chan, 2 * n_slots), F32),
            pltpu.VMEM((2 * n_slots, n_slots), F32),
            pltpu.VMEM((2, n_slots, n_slots), BF16),
            pltpu.VMEM((n_slots, prof), F32),
            sem((n_lines // group,)),
            sem((4,)), sem((4,)), sem, sem, sem((2,)), sem((2,)), sem, sem,
        ],
        compiler_params=pltpu.CompilerParams(
            collective_id=0, has_side_effects=True, vmem_limit_bytes=60 * 1024 * 1024
        ),
    )(columns.T, dep, jacobian, chan_precision, rows, obs_slot[0], counts.reshape(n_lines, 1))
    result = pl.pallas_call(
        spread,
        out_shape=jax.ShapeDtypeStruct((prof, n_cols), F32),
        in_specs=[in_vmem, in_vmem],
        out_specs=in_vmem,
        compiler_params=pltpu.CompilerParams(vmem_limit_bytes=48 * 1024 * 1024),
    )(back, rows)
    return result.T


def solution(mesh):
    placed = (
        P(("band", "lev"), None),
        P("lev", "band", None, None),
        P(),
        P(),
        P(("band", "lev"), None, None),
        P("lev", "band", None),
        P("lev", "band"),
    )
    return jax.shard_map(
        on_device, mesh=mesh, in_specs=placed, out_specs=P(("band", "lev"), None), check_vma=False
    )
```

time: 150 us -> 37.7 us (0.25)
  local copies, waits for them, and re-layouts: 40.7 us -> 3.63 us
  other arithmetic: 35.5 us -> 0 us
  Pallas kernels: 0 us -> 33.8 us
  matrix products: 24.6 us -> 0 us
  waiting for transfers between devices: 17.9 us -> 0 us
  starting transfers between devices: 17.6 us -> 0 us
  blocking collectives: 12.9 us -> 0 us
    pallas_call x0 -> x2, Pallas kernels: none -> 33.8 us  [the longest x1 31.8 us: on_device(): pl.pallas_call(functools.partial(exchange, n_band, n_lev, group), out_sha...]
    scatter-add x2 -> x0, other arithmetic: 28.3 us -> none  [the longest x1 25.2 us: on_device(): jax.ops.segment_sum(obs_adjoint, slot_list, num_segments=n_slots)]
    dot_general x2 -> x0, matrix products: 24.6 us -> none  [the longest x1 16.3 us: on_device(): jnp.dot(residual, chan_precision, preferred_element_type=jnp.float32)]
    gather x2 -> x0, local copies, waits for them, and re-layouts: 17.9 us -> none  [the longest x1 17 us: on_device(): obs_columns = arrived_rows[slot_list]]
    all_to_all x3 -> x0, starting transfers between devices: 13.9 us -> none  [the longest x1 7.25 us: on_device(): lax.all_to_all(outgoing, 'band', split_axis=0, concat_axis=0, tiled=True)]
    all_to_all x1 -> x0, blocking collectives: 12.9 us -> none  [on_device(): lax.all_to_all(adjoint_slots, 'band', split_axis=0, concat_axis=0, tiled=...]
    all_to_all x3 -> x0, waiting for transfers between devices: 11.5 us -> none  [the longest x1 6.37 us: on_device(): lax.all_to_all(outgoing, 'band', split_axis=0, concat_axis=0, tiled=True)]
    convert_element_type x1 -> x0, local copies, waits for them, and re-layouts: 7.65 us -> none  [on_device(): line_deps.reshape(-1, n_chan).astype(jnp.float32)]
  transfers between devices with their start and end apart: 5 -> 0, of which waited for: 3 -> 0; matrix products, arithmetic and copies ran while one was open for 10% -> 0% of each run, Pallas kernels for 0% -> 0%
where the time goes in v1:
time: 37.7 us; the launch traced here: 37.5 us
  Pallas kernels  33.8 us (90%)
  local copies, waits for them, and re-layouts  3.63 us (10%)
    pallas_call x1, Pallas kernels, on_device(): pl.pallas_call(functools.partial(exchange, n_band, n_lev, group), out_sha...  31.8 us
    pallas_call x1, Pallas kernels, on_device(): pl.pallas_call(spread, out_shape=jax.ShapeDtypeStruct((prof, n_cols), F32...  2.02 us
    squeeze x1, local copies, waits for them, and re-layouts, on_device(): rows = send_rows[0]  1.37 us
    reshape x1, local copies, waits for them, and re-layouts, on_device(): counts.reshape(n_lines, 1)  1.34 us
    unnamed x4, local copies, waits for them, and re-layouts  0.92 us

profile of v1, /device:TPU:0, one launch (start us, length us, event | category | flops | bytes accessed | tf_op | source)
XLA Modules:
  0.0 37.5 jit_solution(557759019191387220)
XLA Ops:
  0.0 1.4 %copy.8.rows = s32[32,4]{1,0:T(8,128)} copy(s32[32,4]{0,1:T(4,128)} %bitcast.11) | data formatting | bytes 1024 | tf_op jit(solution)/shard_map/squeeze | solution.py:235
  1.4 1.3 %copy.9.counts = s32[32,1]{1,0:T(8,128)} copy(s32[32,1]{0,1:T(1,128)} %bitcast.12) | data formatting | bytes 256 | tf_op jit(solution)/shard_map/reshape | solution.py:271
  2.7 0.0 copy-start.1
  2.7 31.8 %shard_map.73.back = f32[32,4,274]{2,1,0:T(4,128)} custom-call(bf16[274,2048]{1,0:T(8,128)(2,1)} %bitcast.9, bf16[32,616,128]{2,1,0:T(8,128)(2,1)} %bitcast.8, bf16[274,616]{1,0:T(8,128)(2,1)} %jac.1, bf16[616,616]{1,0:T(8,128)(2,1)} %prec.1, s32[32,4]{1,0:T(8,128)} %copy.8.rows, s32[32,128]{1,0:T(8,128)} %bitcast.10, s32[32,1]{1,0:T(8,128)} %copy.9.counts), custom_call_target="tpu_custom_call" | custom-call | tf_op jit(solution)/shard_map/pallas_call | solution.py:244
  34.5 0.0 copy-done.1
  34.5 0.0 copy-start
  34.5 0.9 %copy-done = f32[32,4,274]{2,1,0:T(4,128)S(1)} copy-done((f32[32,4,274]{2,1,0:T(4,128)S(1)}, f32[32,4,274]{2,1,0:T(4,128)}, u32[]{:S(2)}) %copy-start) | copy-done | bytes 140312
  35.4 2.0 %shard_map.74 = f32[274,2048]{1,0:T(8,128)} custom-call(f32[32,4,274]{2,1,0:T(4,128)S(1)} %copy-done, s32[32,4]{1,0:T(8,128)S(1)} %copy-done.1), custom_call_target="tpu_custom_call" | custom-call | tf_op jit(solution)/shard_map/pallas_call | solution.py:272
Async XLA Ops:
  2.7 31.8 %copy-start.1 = (s32[32,4]{1,0:T(8,128)S(1)}, s32[32,4]{1,0:T(8,128)}, u32[]{:S(2)}) copy-start(s32[32,4]{1,0:T(8,128)} %copy.8.rows) | copy-start | bytes 1540
  34.5 0.9 %copy-start = (f32[32,4,274]{2,1,0:T(4,128)S(1)}, f32[32,4,274]{2,1,0:T(4,128)}, u32[]{:S(2)}) copy-start(f32[32,4,274]{2,1,0:T(4,128)} %shard_map.73.back) | copy-start | bytes 420868

commit v2 on v1

--- a/solution.py
+++ b/solution.py
@@ -30,18 +30,24 @@
     return jnp.where(lax.broadcasted_iota(jnp.int32, (count, row.shape[1]), 0) == row, 1.0, 0.0)
 
 
-def picks(rows_ref, n_cols):
-    n, cap = rows_ref.shape
-    lanes = lax.broadcasted_iota(jnp.int32, (n, n_cols), 1)
+def upright(row):
+    shape = (row.shape[1], row.shape[1])
+    same = lax.broadcasted_iota(jnp.int32, shape, 0) == lax.broadcasted_iota(jnp.int32, shape, 1)
+    return jnp.sum(jnp.where(same, row.astype(F32), 0.0), axis=1, keepdims=True).astype(jnp.int32)
+
+
+def picks(rows_ref, n_cols, first=0):
+    cap, n = rows_ref.shape
+    lanes = lax.broadcasted_iota(jnp.int32, (n, n_cols), 1) + first
     return jnp.concatenate(
-        [jnp.where(lanes == rows_ref[:, c : c + 1], 1.0, 0.0) for c in range(cap)], axis=0
+        [jnp.where(lanes == upright(rows_ref[c : c + 1]), 1.0, 0.0) for c in range(cap)], axis=0
     ).astype(BF16)
 
 
 def exchange(
-    n_band, n_lev, group, cols, dep, jac, prec, rows, slots, counts, back,
-    lines, padded, edge, edge_in, dep_in, wide, sent, got, gotf, mine, mine_in,
-    obs, pair, small, total, dep_sem, entry_out, entry_in, col_out, col_in, row_out, row_in, adj_out, adj_in,
+    n_band, n_lev, group, cols_in, dep, jac_in, prec_in, rows, slots, counts, back,
+    cols, jac, prec, lines, padded, edge, edge_in, dep_in, wide, sent, got, gotf, mine, mine_in,
+    obs, pair, small, total, arg_sem, dep_sem, entry_out, entry_in, col_out, col_in, row_out, row_in, adj_out, adj_in,
 ):
     decay = math.exp(-1.0 / corr_length)
     norm = 1.0 / (1.0 - decay * decay)
@@ -54,6 +60,11 @@
     me = band * n_lev + lev
     has_prev, has_next = band > 0, band < n_band - 1
 
+    fetched = [
+        pltpu.make_async_copy(source, target, arg_sem.at[i])
+        for i, (source, target) in enumerate(((cols_in, cols), (jac_in, jac), (prec_in, prec)))
+    ]
+    fetched[0].start()
     barrier = pltpu.get_barrier_semaphore()
 
     def greet(step, carry):
@@ -73,8 +84,12 @@
 
     for g in range(n_groups):
         load(g).start()
-
-    gathered = across(picks(rows, cols.shape[1]), cols[...])
+    fetched[1].start()
+    fetched[2].start()
+
+    chosen = picks(rows, cols.shape[1])
+    fetched[0].wait()
+    gathered = across(chosen, cols[...])
     for c in range(cap):
         wide[:, c, :] = gathered[c * n : (c + 1) * n]
     sent[...] = wide[...].astype(BF16)
@@ -83,7 +98,7 @@
     numbers = slots[...]
     ordered = lax.rem(numbers, cap) * n + lax.div(numbers, cap)
     place = lax.broadcasted_iota(jnp.int32, (n_lines, n_pos), 1)
-    ordered = jnp.where(place < counts[...], ordered, -1)
+    ordered = jnp.where(place < upright(counts[...]), ordered, -1)
     nothing = jnp.full((8, n_pos), -1, jnp.int32)
     padded[0:8] = nothing
     padded[8 : 8 + n_lines] = ordered
@@ -156,7 +171,16 @@
         pair[...] += across(weights, own)
         return carry
 
-    lax.fori_loop(0, n_groups, add_group, 0)
+    early = n_groups - n_groups // 4
+    lax.fori_loop(0, early, add_group, 0)
+    settle(got, col_in)
+    gotf[...] = got[...].astype(F32)
+    mine[...] = jnp.concatenate([gotf[:, c, :] for c in range(cap)], axis=0).astype(BF16)
+    for to, there in neighbours:
+        @pl.when(there)
+        def _(to=to):
+            columns_to(to).start()
+    lax.fori_loop(early, n_groups, add_group, 0)
 
     obs[:, :n_slots] = inner * obs[:, :n_slots] - side * obs[:, n_slots:]
     pair[:n_slots] = inner * pair[:n_slots] - side * pair[n_slots:]
@@ -183,6 +207,9 @@
             obs[:, :n_slots] -= side * across(dep_in[at], mask)
             small[at] = across(mask, hot(theirs, n_slots).astype(BF16)).astype(BF16)
 
+    fetched[1].wait()
+    fetched[2].wait()
+
     def two(left, value):
         both = plain(left, jnp.concatenate(halves(value), axis=1))
         width = value.shape[1]
@@ -193,13 +220,6 @@
     metric_high, metric_low = halves(plain(jac[...], high) + plain(jac[...], low))
     pair_high, pair_low = halves(pair[:n_slots])
 
-    settle(got, col_in)
-    gotf[...] = got[...].astype(F32)
-    mine[...] = jnp.concatenate([gotf[:, c, :] for c in range(cap)], axis=0).astype(BF16)
-    for to, there in neighbours:
-        @pl.when(there)
-        def _(to=to):
-            columns_to(to).start()
     block = mine[...]
     total[...] = plain(pair_high, block) + plain(pair_low, block)
     for at, there in neighbours:
@@ -221,32 +241,48 @@
     settle(wide, adj_out)
 
 
-def spread(back, rows, out):
-    n, cap = rows.shape
+def spread(back_in, rows, out, back, piece, in_sem, out_sem):
+    fetch = pltpu.make_async_copy(back_in, back, in_sem)
+    fetch.start()
+    cap = rows.shape[0]
+    parts, _, width = piece.shape
+    chosen = [picks(rows, width, part * width) for part in range(parts)]
+    fetch.wait()
     values = jnp.concatenate([back[:, c, :] for c in range(cap)], axis=0).T
-    chosen = picks(rows, out.shape[1])
-    high, low = halves(values)
-    out[...] = plain(jnp.concatenate([high, low], axis=1), jnp.concatenate([chosen, chosen], axis=0))
+    values = jnp.concatenate(halves(values), axis=1)
+    copies = []
+    for part in range(parts):
+        piece[part] = plain(values, jnp.concatenate([chosen[part], chosen[part]], axis=0))
+        copies.append(
+            pltpu.make_async_copy(piece.at[part], out.at[:, part * width : (part + 1) * width], out_sem.at[part])
+        )
+        copies[part].start()
+    for copy in copies:
+        copy.wait()
 
 
 def on_device(columns, departures, jacobian, chan_precision, send_rows, obs_slot, counts):
     n_band, n_lev = lax.axis_size("band"), lax.axis_size("lev")
     n = n_band * n_lev
-    rows = send_rows[0]
-    cap = rows.shape[1]
+    rows = send_rows[0].T
+    cap = rows.shape[0]
     n_slots = n * cap
     n_cols, prof = columns.shape
     dep = departures[0].transpose(0, 2, 1)
     n_lines, n_chan, n_pos = dep.shape
-    group = 8
+    group, parts = 8, 4
     in_vmem = pl.BlockSpec(memory_space=pltpu.VMEM)
+    anywhere = pl.BlockSpec(memory_space=pl.ANY)
     sem = pltpu.SemaphoreType.DMA
     back = pl.pallas_call(
         functools.partial(exchange, n_band, n_lev, group),
         out_shape=jax.ShapeDtypeStruct((n, cap, prof), F32),
-        in_specs=[in_vmem, pl.BlockSpec(memory_space=pl.ANY)] + [in_vmem] * 5,
+        in_specs=[anywhere] * 4 + [in_vmem] * 3,
         out_specs=in_vmem,
         scratch_shapes=[
+            pltpu.VMEM((prof, n_cols), BF16),
+            pltpu.VMEM((prof, n_chan), BF16),
+            pltpu.VMEM((n_chan, n_chan), BF16),
             pltpu.VMEM((n_lines, n_chan, n_pos), BF16),
             pltpu.VMEM((n_lines + 16, n_pos), jnp.int32),
             pltpu.VMEM((2, 8, n_pos), jnp.int32),
@@ -262,19 +298,26 @@
             pltpu.VMEM((2 * n_slots, n_slots), F32),
             pltpu.VMEM((2, n_slots, n_slots), BF16),
             pltpu.VMEM((n_slots, prof), F32),
+            sem((3,)),
             sem((n_lines // group,)),
             sem((4,)), sem((4,)), sem, sem, sem((2,)), sem((2,)), sem, sem,
         ],
         compiler_params=pltpu.CompilerParams(
             collective_id=0, has_side_effects=True, vmem_limit_bytes=60 * 1024 * 1024
         ),
-    )(columns.T, dep, jacobian, chan_precision, rows, obs_slot[0], counts.reshape(n_lines, 1))
+    )(columns.T, dep, jacobian, chan_precision, rows, obs_slot[0], counts)
     result = pl.pallas_call(
         spread,
         out_shape=jax.ShapeDtypeStruct((prof, n_cols), F32),
-        in_specs=[in_vmem, in_vmem],
-        out_specs=in_vmem,
-        compiler_params=pltpu.CompilerParams(vmem_limit_bytes=48 * 1024 * 1024),
+        in_specs=[anywhere, in_vmem],
+        out_specs=anywhere,
+        scratch_shapes=[
+            pltpu.VMEM((n, cap, prof), F32),
+            pltpu.VMEM((parts, prof, n_cols // parts), F32),
+            sem,
+            sem((parts,)),
+        ],
+        compiler_params=pltpu.CompilerParams(vmem_limit_bytes=60 * 1024 * 1024),
     )(back, rows)
     return result.T
 

time: 37.7 us -> 31.5 us (0.84)
  local copies, waits for them, and re-layouts: 3.63 us -> 0 us
  Pallas kernels: 33.8 us -> 31.2 us
    pallas_call x1, Pallas kernels: 31.8 us -> 27.9 us  [on_device(): pl.pallas_call(functools.partial(exchange, n_band, n_lev, group), out_sha...]
    squeeze x1 -> x0, local copies, waits for them, and re-layouts: 1.37 us -> none  [on_device(): rows = send_rows[0]]
    reshape x1 -> x0, local copies, waits for them, and re-layouts: 1.34 us -> none  [on_device(): counts.reshape(n_lines, 1)]
    pallas_call x1, Pallas kernels: 2.02 us -> 3.33 us  [on_device(): pl.pallas_call(spread, out_shape=jax.ShapeDtypeStruct((prof, n_cols), F32...]
    unnamed x4 -> x0, local copies, waits for them, and re-layouts: 0.92 us -> none
where the time goes in v2:
time: 31.5 us; the launch traced here: 31.2 us
  Pallas kernels  31.2 us (99%)
    pallas_call x1, Pallas kernels, on_device(): pl.pallas_call(functools.partial(exchange, n_band, n_lev, group), out_sha...  27.9 us
    pallas_call x1, Pallas kernels, on_device(): pl.pallas_call(spread, out_shape=jax.ShapeDtypeStruct((prof, n_cols), F32...  3.33 us

profile of v2, /device:TPU:0, one launch (start us, length us, event | category | flops | bytes accessed | tf_op | source)
XLA Modules:
  0.0 31.2 jit_solution(12821540277767236377)
XLA Ops:
  0.0 27.9 %shard_map.73.back_in = f32[32,4,274]{2,1,0:T(4,128)} custom-call(bf16[274,2048]{1,0:T(8,128)(2,1)} %bitcast.10, bf16[32,616,128]{2,1,0:T(8,128)(2,1)} %bitcast.9, bf16[274,616]{1,0:T(8,128)(2,1)} %jac_in.1, bf16[616,616]{1,0:T(8,128)(2,1)} %prec_in.1, s32[4,32]{1,0:T(4,128)} %bitcast.12, s32[32,128]{1,0:T(8,128)} %bitcast.11, s32[1,32]{1,0:T(1,128)} %counts.1), custom_call_target="tpu_custom_call" | custom-call | tf_op jit(solution)/shard_map/pallas_call | solution.py:277
  27.9 3.3 %shard_map.74 = f32[274,2048]{1,0:T(8,128)} custom-call(f32[32,4,274]{2,1,0:T(4,128)} %shard_map.73.back_in, s32[4,32]{1,0:T(4,128)} %bitcast.13), custom_call_target="tpu_custom_call" | custom-call | tf_op jit(solution)/shard_map/pallas_call | solution.py:309

commit v3 on v2

--- a/solution.py
+++ b/solution.py
@@ -36,12 +36,13 @@
     return jnp.sum(jnp.where(same, row.astype(F32), 0.0), axis=1, keepdims=True).astype(jnp.int32)
 
 
-def picks(rows_ref, n_cols, first=0):
-    cap, n = rows_ref.shape
-    lanes = lax.broadcasted_iota(jnp.int32, (n, n_cols), 1) + first
-    return jnp.concatenate(
-        [jnp.where(lanes == upright(rows_ref[c : c + 1]), 1.0, 0.0) for c in range(cap)], axis=0
-    ).astype(BF16)
+def columns_of(rows_ref):
+    return jnp.concatenate([upright(rows_ref[c : c + 1]) for c in range(rows_ref.shape[0])], axis=0)
+
+
+def picks(wanted, n_cols, first=0):
+    lanes = lax.broadcasted_iota(jnp.int32, (wanted.shape[0], n_cols), 1)
+    return jnp.where(lanes == wanted - first, 1.0, 0.0).astype(BF16)
 
 
 def exchange(
@@ -87,7 +88,7 @@
     fetched[1].start()
     fetched[2].start()
 
-    chosen = picks(rows, cols.shape[1])
+    chosen = picks(columns_of(rows), cols.shape[1])
     fetched[0].wait()
     gathered = across(chosen, cols[...])
     for c in range(cap):
@@ -175,7 +176,8 @@
     lax.fori_loop(0, early, add_group, 0)
     settle(got, col_in)
     gotf[...] = got[...].astype(F32)
-    mine[...] = jnp.concatenate([gotf[:, c, :] for c in range(cap)], axis=0).astype(BF16)
+    arrived = jnp.concatenate([gotf[:, c, :] for c in range(cap)], axis=0)
+    mine[...] = arrived.T.astype(BF16)
     for to, there in neighbours:
         @pl.when(there)
         def _(to=to):
@@ -221,13 +223,13 @@
     pair_high, pair_low = halves(pair[:n_slots])
 
     block = mine[...]
-    total[...] = plain(pair_high, block) + plain(pair_low, block)
+    total[...] = across(pair_high, block) + across(pair_low, block)
     for at, there in neighbours:
         @pl.when(there)
         def _(at=at):
             columns_to(at).wait_send()
             pltpu.make_async_copy(mine_in.at[at], mine_in.at[at], row_in.at[at]).wait()
-            total[...] -= side * plain(small[at], mine_in[at])
+            total[...] -= side * across(small[at], mine_in[at])
     mixed_high, mixed_low = halves(total[...])
     adjoint = (
         plain(mixed_high, metric_high) + (plain(mixed_low, metric_high) + plain(mixed_high, metric_low)) - measured
@@ -246,7 +248,8 @@
     fetch.start()
     cap = rows.shape[0]
     parts, _, width = piece.shape
-    chosen = [picks(rows, width, part * width) for part in range(parts)]
+    wanted = columns_of(rows)
+    chosen = [picks(wanted, width, part * width) for part in range(parts)]
     fetch.wait()
     values = jnp.concatenate([back[:, c, :] for c in range(cap)], axis=0).T
     values = jnp.concatenate(halves(values), axis=1)
@@ -270,7 +273,7 @@
     n_cols, prof = columns.shape
     dep = departures[0].transpose(0, 2, 1)
     n_lines, n_chan, n_pos = dep.shape
-    group, parts = 8, 4
+    group, parts = 8, 2
     in_vmem = pl.BlockSpec(memory_space=pltpu.VMEM)
     anywhere = pl.BlockSpec(memory_space=pl.ANY)
     sem = pltpu.SemaphoreType.DMA
@@ -292,8 +295,8 @@
             pltpu.VMEM((n, cap, prof), BF16),
             pltpu.VMEM((n, cap, prof), BF16),
             pltpu.VMEM((n, cap, prof), F32),
-            pltpu.VMEM((n_slots, prof), BF16),
-            pltpu.VMEM((2, n_slots, prof), BF16),
+            pltpu.VMEM((prof, n_slots), BF16),
+            pltpu.VMEM((2, prof, n_slots), BF16),
             pltpu.VMEM((n_chan, 2 * n_slots), F32),
             pltpu.VMEM((2 * n_slots, n_slots), F32),
             pltpu.VMEM((2, n_slots, n_slots), BF16),

time: 31.5 us -> 31 us (0.984)
  Pallas kernels: 31.2 us -> 30.8 us
    pallas_call x1, Pallas kernels: 27.9 us -> 27.4 us  [on_device(): pl.pallas_call(functools.partial(exchange, n_band, n_lev, group), out_sha...]
where the time goes in v3:
time: 31 us; the launch traced here: 30.8 us
  Pallas kernels  30.8 us (99%)
    pallas_call x1, Pallas kernels, on_device(): pl.pallas_call(functools.partial(exchange, n_band, n_lev, group), out_sha...  27.4 us
    pallas_call x1, Pallas kernels, on_device(): pl.pallas_call(spread, out_shape=jax.ShapeDtypeStruct((prof, n_cols), F32...  3.4 us

profile of v3, /device:TPU:0, one launch (start us, length us, event | category | flops | bytes accessed | tf_op | source)
XLA Modules:
  0.0 30.8 jit_solution(6756387408133169036)
XLA Ops:
  0.0 27.4 %shard_map.73.back_in = f32[32,4,274]{2,1,0:T(4,128)} custom-call(bf16[274,2048]{1,0:T(8,128)(2,1)} %bitcast.10, bf16[32,616,128]{2,1,0:T(8,128)(2,1)} %bitcast.9, bf16[274,616]{1,0:T(8,128)(2,1)} %jac_in.1, bf16[616,616]{1,0:T(8,128)(2,1)} %prec_in.1, s32[4,32]{1,0:T(4,128)} %bitcast.12, s32[32,128]{1,0:T(8,128)} %bitcast.11, s32[1,32]{1,0:T(1,128)} %counts.1), custom_call_target="tpu_custom_call" | custom-call | tf_op jit(solution)/shard_map/pallas_call | solution.py:280
  27.4 3.4 %shard_map.74 = f32[274,2048]{1,0:T(8,128)} custom-call(f32[32,4,274]{2,1,0:T(4,128)} %shard_map.73.back_in, s32[4,32]{1,0:T(4,128)} %bitcast.13), custom_call_target="tpu_custom_call" | custom-call | tf_op jit(solution)/shard_map/pallas_call | solution.py:312
